TPU v7x, 512 devices: a whole 4x4x16 slice. The times are simulated.
512 devices in a mesh: band: 16 (over z_hi, y), fft: 32 (over x, z_lo, core).
Axes of the slice: x: 4, y: 4, z: 16 (z_hi: 4, z_lo: 4; z = z_hi * 4 + z_lo), core: 2. Of those that a mesh axis runs over, the one named last changes fastest.
Arguments:
- orbitals: bfloat16 [64, 128, 128, 128], P('band', 'fft'), may hold values from -6 to 6
- kernel: float32 [128, 128, 128], P(None, 'fft'), may hold values from 0.05 to 2, as said below
- pairing: int32 [16, 4], P('band'), may hold values from 0 to 3, each once within a row
- owner: int32 [1], replicated, may hold values from 0 to 65535
Outputs:
- exchange: float32 [64, 128, 128, 128], P('band', 'fft')
Inputs may be any that keep to these rules, and one draw needn't show every extreme that they name: Each row of pairing is a permutation of 0 to 3. kernel is symmetric under k -> -k: kernel[kz, ky, kx] = kernel[(-kz) mod 128, (-ky) mod 128, (-kx) mod 128].
All inputs are finite; a program needn't handle non-finite values.
Results may differ from a plain program's by a relative error of at most 0.0005.
Values may be sent and summed in bfloat16 or wider, within the bound.
A program may use at most 64 MiB of HBM per device.

v0:
```python
import math

import jax
import jax.numpy as jnp
from jax import lax
from jax.sharding import PartitionSpec as P

HIGH = lax.Precision.HIGHEST


def broadcast(value, axis, root):
    mine = lax.axis_index(axis) == root
    return lax.psum(jnp.where(mine, value, jnp.zeros_like(value)), axis)


def tables(length):
    counter = jnp.arange(length, dtype=jnp.int32)
    phase = (jnp.outer(counter, counter) % length).astype(jnp.float32) * (2.0 * math.pi / length)
    return (jnp.cos(phase), jnp.sin(phase))


def along(form, field, table):
    return jnp.einsum(form, field, table, precision=HIGH)


def forward_pair(real_part, imag_part, form, cosine_table, sine_table):
    new_real = along(form, real_part, cosine_table) + along(form, imag_part, sine_table)
    new_imag = along(form, imag_part, cosine_table) - along(form, real_part, sine_table)
    return (new_real, new_imag)


def inverse_pair(real_part, imag_part, form, cosine_table, sine_table, scale):
    new_real = (along(form, real_part, cosine_table) - along(form, imag_part, sine_table)) * scale
    new_imag = (along(form, imag_part, cosine_table) + along(form, real_part, sine_table)) * scale
    return (new_real, new_imag)


def middle_section(real_part, imag_part, kernel, cosine_table, sine_table):
    scale = 1.0 / cosine_table.shape[0]
    form_y = "pzyx,yk->pzkx"
    form_z = "pzyx,zk->pkyx"
    real_part, imag_part = forward_pair(real_part, imag_part, form_y, cosine_table, sine_table)
    real_part, imag_part = (
        lax.all_to_all(real_part, "fft", split_axis=2, concat_axis=1, tiled=True),
        lax.all_to_all(imag_part, "fft", split_axis=2, concat_axis=1, tiled=True),
    )
    real_part, imag_part = forward_pair(real_part, imag_part, form_z, cosine_table, sine_table)
    real_part = real_part * kernel[None]
    imag_part = imag_part * kernel[None]
    real_part, imag_part = inverse_pair(
        real_part, imag_part, form_z, cosine_table, sine_table, scale
    )
    real_part, imag_part = (
        lax.all_to_all(real_part, "fft", split_axis=1, concat_axis=2, tiled=True),
        lax.all_to_all(imag_part, "fft", split_axis=1, concat_axis=2, tiled=True),
    )
    return inverse_pair(real_part, imag_part, form_y, cosine_table, sine_table, scale)


def potential_real(density, kernel, cosine_table, sine_table):
    scale = 1.0 / cosine_table.shape[0]
    form_x = "pzyx,xk->pzyk"
    real_part = along(form_x, density, cosine_table)
    imag_part = -along(form_x, density, sine_table)
    real_part, imag_part = middle_section(real_part, imag_part, kernel, cosine_table, sine_table)
    return (along(form_x, real_part, cosine_table) - along(form_x, imag_part, sine_table)) * scale


def local(orbitals, kernel, pairing, owner):
    root_group = owner[0] % lax.axis_size("band")
    orbital_block = broadcast(orbitals, "band", root_group)
    partner = jnp.take(orbital_block, pairing[0], axis=0).astype(jnp.float32)
    density = partner * orbitals.astype(jnp.float32)
    cosine_table, sine_table = tables(orbitals.shape[3])
    width = 1
    pieces = []
    for pair_index in range(0, density.shape[0], width):
        pieces.append(
            potential_real(
                density[pair_index : pair_index + width], kernel, cosine_table, sine_table
            )
        )
    field = jnp.concatenate(pieces, axis=0)
    return -(partner * field)


def solution(mesh):
    placed = (P("band", "fft", None, None), P(None, "fft", None), P("band", None), P())
    return jax.shard_map(
        local, mesh=mesh, in_specs=placed, out_specs=P("band", "fft", None, None), check_vma=False
    )
```

profile of v0, /device:TPU:1, one launch (start us, length us, event | category | flops | bytes accessed | tf_op | source)
XLA Modules:
  0.0 486.0 jit_solution(18159494735130517934)
XLA Ops:
  8.7 200.5 %all-reduce.2.cloned.1.call-done = bf16[4,4,128,128]{3,2,1,0:T(8,128)(2,1)} async-done(((bf16[4,4,128,128]{3,2,1,0:T(8,128)(2,1)}), bf16[4,4,128,128]{3,2,1,0:T(8,128)(2,1)}) %all-reduce.2.cloned.1.call-update) | async-done | bytes 524304 | tf_op jit(solution)/shard_map/psum | solution.py:13
  209.2 1.7 gather_fusion
  214.6 16.5 %all-to-all-start.1 = ((f32[1,4,128,128]{3,1,0,2:T(4,128)}), f32[1,4,128,128]{3,1,0,2:T(4,128)S(1)}, u32[]{:S(2)}, u32[]{:S(2)}) async-start(f32[1,4,128,128]{3,1,0,2:T(4,128)} %copy.100), calls=%async_computation.1 | async-start | bytes 524288 | tf_op jit(solution)/shard_map/all_to_all | solution.py:45
  233.3 9.1 %all-to-all-done.1 = f32[1,4,128,128]{3,1,0,2:T(4,128)S(1)} async-done(((f32[1,4,128,128]{3,1,0,2:T(4,128)}), f32[1,4,128,128]{3,1,0,2:T(4,128)S(1)}, u32[]{:S(2)}, u32[]{:S(2)}) %all-to-all-start.1) | async-done | bytes 262176 | tf_op jit(solution)/shard_map/all_to_all | solution.py:45
  242.4 3.7 all-to-all-start
  249.5 7.9 %all-to-all-done = f32[1,4,128,128]{3,1,0,2:T(4,128)S(1)} async-done(((f32[1,4,128,128]{3,1,0,2:T(4,128)}), f32[1,4,128,128]{3,1,0,2:T(4,128)S(1)}, u32[]{:S(2)}, u32[]{:S(2)}) %all-to-all-start) | async-done | bytes 262176 | tf_op jit(solution)/shard_map/all_to_all | solution.py:44
  258.1 3.7 all-to-all-start.5
  264.0 9.1 %all-to-all-done.5 = f32[1,4,128,128]{3,1,0,2:T(4,128)S(1)} async-done(((f32[1,4,128,128]{3,1,0,2:T(4,128)}), f32[1,4,128,128]{3,1,0,2:T(4,128)S(1)}, u32[]{:S(2)}, u32[]{:S(2)}) %all-to-all-start.5) | async-done | bytes 262176 | tf_op jit(solution)/shard_map/all_to_all | solution.py:45
  273.1 3.9 all-to-all-start.4
  280.4 7.8 %all-to-all-done.4 = f32[1,4,128,128]{3,1,0,2:T(4,128)S(1)} async-done(((f32[1,4,128,128]{3,1,0,2:T(4,128)}), f32[1,4,128,128]{3,1,0,2:T(4,128)S(1)}, u32[]{:S(2)}, u32[]{:S(2)}) %all-to-all-start.4) | async-done | bytes 262176 | tf_op jit(solution)/shard_map/all_to_all | solution.py:44
  288.3 3.7 all-to-all-start.9
  294.1 9.1 %all-to-all-done.9 = f32[1,4,128,128]{3,1,0,2:T(4,128)S(1)} async-done(((f32[1,4,128,128]{3,1,0,2:T(4,128)}), f32[1,4,128,128]{3,1,0,2:T(4,128)S(1)}, u32[]{:S(2)}, u32[]{:S(2)}) %all-to-all-start.9) | async-done | bytes 262176 | tf_op jit(solution)/shard_map/all_to_all | solution.py:45
  303.2 3.7 all-to-all-start.8
  309.5 0.9 copy.178
  310.4 7.9 %all-to-all-done.8 = f32[1,4,128,128]{3,1,0,2:T(4,128)S(1)} async-done(((f32[1,4,128,128]{3,1,0,2:T(4,128)}), f32[1,4,128,128]{3,1,0,2:T(4,128)S(1)}, u32[]{:S(2)}, u32[]{:S(2)}) %all-to-all-start.8) | async-done | bytes 262176 | tf_op jit(solution)/shard_map/all_to_all | solution.py:44
  318.9 3.7 all-to-all-start.13
  324.8 0.9 copy-done.8
  327.4 6.5 %all-to-all-done.13 = f32[1,4,128,128]{3,1,0,2:T(4,128)S(1)} async-done(((f32[1,4,128,128]{3,1,0,2:T(4,128)}), f32[1,4,128,128]{3,1,0,2:T(4,128)S(1)}, u32[]{:S(2)}, u32[]{:S(2)}) %all-to-all-start.13) | async-done | bytes 262176 | tf_op jit(solution)/shard_map/all_to_all | solution.py:45
  333.9 4.1 all-to-all-start.12
  340.7 0.9 copy.114
  342.2 7.1 %all-to-all-done.12 = f32[1,4,128,128]{3,1,0,2:T(4,128)S(1)} async-done(((f32[1,4,128,128]{3,1,0,2:T(4,128)}), f32[1,4,128,128]{3,1,0,2:T(4,128)S(1)}, u32[]{:S(2)}, u32[]{:S(2)}) %all-to-all-start.12) | async-done | bytes 262176 | tf_op jit(solution)/shard_map/all_to_all | solution.py:44
  350.0 3.7 all-to-all-start.3
  354.3 0.9 copy.109
  358.0 7.0 %all-to-all-done.3 = f32[1,128,4,128]{3,2,0,1:T(4,128)S(1)} async-done(((f32[1,128,4,128]{3,2,0,1:T(4,128)}), f32[1,128,4,128]{3,2,0,1:T(4,128)S(1)}, u32[]{:S(2)}, u32[]{:S(2)}) %all-to-all-start.3) | async-done | bytes 262176 | tf_op jit(solution)/shard_map/all_to_all | solution.py:55
  364.9 3.7 all-to-all-start.2
  369.9 0.9 copy.140
  370.9 0.9 copy-done.6
  373.1 1.3 fusion.130
  374.5 5.5 %all-to-all-done.2 = f32[1,128,4,128]{3,2,0,1:T(4,128)S(1)} async-done(((f32[1,128,4,128]{3,2,0,1:T(4,128)}), f32[1,128,4,128]{3,2,0,1:T(4,128)S(1)}, u32[]{:S(2)}, u32[]{:S(2)}) %all-to-all-start.2) | async-done | bytes 262176 | tf_op jit(solution)/shard_map/all_to_all | solution.py:54
  379.9 3.9 all-to-all-start.7
  384.5 0.9 copy.135
  388.3 6.8 %all-to-all-done.7 = f32[1,128,4,128]{3,2,0,1:T(4,128)S(1)} async-done(((f32[1,128,4,128]{3,2,0,1:T(4,128)}), f32[1,128,4,128]{3,2,0,1:T(4,128)S(1)}, u32[]{:S(2)}, u32[]{:S(2)}) %all-to-all-start.7) | async-done | bytes 262176 | tf_op jit(solution)/shard_map/all_to_all | solution.py:55
  395.1 3.7 all-to-all-start.6
  400.3 0.9 copy-done.4
  401.9 1.4 fusion.114
  404.6 5.5 %all-to-all-done.6 = f32[1,128,4,128]{3,2,0,1:T(4,128)S(1)} async-done(((f32[1,128,4,128]{3,2,0,1:T(4,128)}), f32[1,128,4,128]{3,2,0,1:T(4,128)S(1)}, u32[]{:S(2)}, u32[]{:S(2)}) %all-to-all-start.6) | async-done | bytes 262176 | tf_op jit(solution)/shard_map/all_to_all | solution.py:54
  410.0 3.7 all-to-all-start.11
  414.4 0.9 copy.161
  420.5 4.5 all-to-all-done.11
  425.0 3.9 all-to-all-start.10
  432.4 7.8 %all-to-all-done.10 = f32[1,128,4,128]{3,2,0,1:T(4,128)S(1)} async-done(((f32[1,128,4,128]{3,2,0,1:T(4,128)}), f32[1,128,4,128]{3,2,0,1:T(4,128)S(1)}, u32[]{:S(2)}, u32[]{:S(2)}) %all-to-all-start.10) | async-done | bytes 262176 | tf_op jit(solution)/shard_map/all_to_all | solution.py:54
  440.2 3.7 all-to-all-start.15
  447.2 8.0 %all-to-all-done.15 = f32[1,128,4,128]{3,2,0,1:T(4,128)S(1)} async-done(((f32[1,128,4,128]{3,2,0,1:T(4,128)}), f32[1,128,4,128]{3,2,0,1:T(4,128)S(1)}, u32[]{:S(2)}, u32[]{:S(2)}) %all-to-all-start.15) | async-done | bytes 262176 | tf_op jit(solution)/shard_map/all_to_all | solution.py:55
  455.2 4.7 all-to-all-start.14
  460.5 1.4 fusion.104
  463.9 7.2 %all-to-all-done.14 = f32[1,128,4,128]{3,2,0,1:T(4,128)} async-done(((f32[1,128,4,128]{3,2,0,1:T(4,128)}), f32[1,128,4,128]{3,2,0,1:T(4,128)}, u32[]{:S(2)}, u32[]{:S(2)}) %all-to-all-start.14) | async-done | bytes 262176 | tf_op jit(solution)/shard_map/all_to_all | solution.py:54
  471.1 1.0 copy.188
  477.5 1.2 fusion.56
  (130 shorter events, 63.8 us)
Async XLA Ops:
  6.5 202.7 %all-reduce.2.cloned.1.call-start = ((), (), s32[]{:S(2)}) async-start(), calls=%async_computation.16 | async-start | bytes 1048576 | tf_op jit(solution)/shard_map/psum | solution.py:13
  8.0 0.7 copy-start.11
  8.7 202.2 %copy-start.1 = (bf16[4,4,128,128]{3,2,1,0:T(8,128)(2,1)S(1)}, bf16[4,4,128,128]{3,2,1,0:T(8,128)(2,1)}, u32[]{:S(2)}) copy-start(bf16[4,4,128,128]{3,2,1,0:T(8,128)(2,1)} %param.4) | copy-start | bytes 1572868
  214.6 27.8 %all-to-all-start.1 = ((f32[1,4,128,128]{3,1,0,2:T(4,128)}), f32[1,4,128,128]{3,1,0,2:T(4,128)S(1)}, u32[]{:S(2)}, u32[]{:S(2)}) async-start(f32[1,4,128,128]{3,1,0,2:T(4,128)} %copy.100), calls=%async_computation.1 | async-start | bytes 524288 | tf_op jit(solution)/shard_map/all_to_all | solution.py:45
  242.4 15.0 %all-to-all-start = ((f32[1,4,128,128]{3,1,0,2:T(4,128)}), f32[1,4,128,128]{3,1,0,2:T(4,128)S(1)}, u32[]{:S(2)}, u32[]{:S(2)}) async-start(f32[1,4,128,128]{3,1,0,2:T(4,128)} %copy.95), calls=%async_computation | async-start | bytes 524288 | tf_op jit(solution)/shard_map/all_to_all | solution.py:44
  257.4 0.7 copy-start.7
  258.1 15.0 %all-to-all-start.5 = ((f32[1,4,128,128]{3,1,0,2:T(4,128)}), f32[1,4,128,128]{3,1,0,2:T(4,128)S(1)}, u32[]{:S(2)}, u32[]{:S(2)}) async-start(f32[1,4,128,128]{3,1,0,2:T(4,128)} %copy.126), calls=%async_computation.5 | async-start | bytes 524288 | tf_op jit(solution)/shard_map/all_to_all | solution.py:45
  273.1 15.2 %all-to-all-start.4 = ((f32[1,4,128,128]{3,1,0,2:T(4,128)}), f32[1,4,128,128]{3,1,0,2:T(4,128)S(1)}, u32[]{:S(2)}, u32[]{:S(2)}) async-start(f32[1,4,128,128]{3,1,0,2:T(4,128)} %copy.121), calls=%async_computation.4 | async-start | bytes 524288 | tf_op jit(solution)/shard_map/all_to_all | solution.py:44
  288.3 15.0 %all-to-all-start.9 = ((f32[1,4,128,128]{3,1,0,2:T(4,128)}), f32[1,4,128,128]{3,1,0,2:T(4,128)S(1)}, u32[]{:S(2)}, u32[]{:S(2)}) async-start(f32[1,4,128,128]{3,1,0,2:T(4,128)} %copy.152), calls=%async_computation.9 | async-start | bytes 524288 | tf_op jit(solution)/shard_map/all_to_all | solution.py:45
  303.2 15.0 %all-to-all-start.8 = ((f32[1,4,128,128]{3,1,0,2:T(4,128)}), f32[1,4,128,128]{3,1,0,2:T(4,128)S(1)}, u32[]{:S(2)}, u32[]{:S(2)}) async-start(f32[1,4,128,128]{3,1,0,2:T(4,128)} %copy.147), calls=%async_computation.8 | async-start | bytes 524288 | tf_op jit(solution)/shard_map/all_to_all | solution.py:44
  318.2 0.7 copy-start.5
  318.9 15.0 %all-to-all-start.13 = ((f32[1,4,128,128]{3,1,0,2:T(4,128)}), f32[1,4,128,128]{3,1,0,2:T(4,128)S(1)}, u32[]{:S(2)}, u32[]{:S(2)}) async-start(f32[1,4,128,128]{3,1,0,2:T(4,128)} %copy.178), calls=%async_computation.13 | async-start | bytes 524288 | tf_op jit(solution)/shard_map/all_to_all | solution.py:45
  324.8 0.9 copy-start.8
  325.8 1.0 copy-start
  333.9 15.4 %all-to-all-start.12 = ((f32[1,4,128,128]{3,1,0,2:T(4,128)}), f32[1,4,128,128]{3,1,0,2:T(4,128)S(1)}, u32[]{:S(2)}, u32[]{:S(2)}) async-start(f32[1,4,128,128]{3,1,0,2:T(4,128)} %copy.173), calls=%async_computation.12 | async-start | bytes 524288 | tf_op jit(solution)/shard_map/all_to_all | solution.py:44
  349.3 0.7 copy-start.3
  350.0 15.0 %all-to-all-start.3 = ((f32[1,128,4,128]{3,2,0,1:T(4,128)}), f32[1,128,4,128]{3,2,0,1:T(4,128)S(1)}, u32[]{:S(2)}, u32[]{:S(2)}) async-start(f32[1,128,4,128]{3,2,0,1:T(4,128)} %copy.114), calls=%async_computation.3 | async-start | bytes 524288 | tf_op jit(solution)/shard_map/all_to_all | solution.py:55
  364.9 15.0 %all-to-all-start.2 = ((f32[1,128,4,128]{3,2,0,1:T(4,128)}), f32[1,128,4,128]{3,2,0,1:T(4,128)S(1)}, u32[]{:S(2)}, u32[]{:S(2)}) async-start(f32[1,128,4,128]{3,2,0,1:T(4,128)} %copy.109), calls=%async_computation.2 | async-start | bytes 524288 | tf_op jit(solution)/shard_map/all_to_all | solution.py:54
  370.8 0.9 copy-start.6
  379.9 15.1 %all-to-all-start.7 = ((f32[1,128,4,128]{3,2,0,1:T(4,128)}), f32[1,128,4,128]{3,2,0,1:T(4,128)S(1)}, u32[]{:S(2)}, u32[]{:S(2)}) async-start(f32[1,128,4,128]{3,2,0,1:T(4,128)} %copy.140), calls=%async_computation.7 | async-start | bytes 524288 | tf_op jit(solution)/shard_map/all_to_all | solution.py:55
  386.0 1.0 copy-start.9
  395.1 15.0 %all-to-all-start.6 = ((f32[1,128,4,128]{3,2,0,1:T(4,128)}), f32[1,128,4,128]{3,2,0,1:T(4,128)S(1)}, u32[]{:S(2)}, u32[]{:S(2)}) async-start(f32[1,128,4,128]{3,2,0,1:T(4,128)} %copy.135), calls=%async_computation.6 | async-start | bytes 524288 | tf_op jit(solution)/shard_map/all_to_all | solution.py:54
  400.3 0.9 copy-start.4
  410.0 15.0 %all-to-all-start.11 = ((f32[1,128,4,128]{3,2,0,1:T(4,128)}), f32[1,128,4,128]{3,2,0,1:T(4,128)S(1)}, u32[]{:S(2)}, u32[]{:S(2)}) async-start(f32[1,128,4,128]{3,2,0,1:T(4,128)} %copy.166), calls=%async_computation.11 | async-start | bytes 524288 | tf_op jit(solution)/shard_map/all_to_all | solution.py:55
  414.4 1.0 copy-start.10
  425.0 15.2 %all-to-all-start.10 = ((f32[1,128,4,128]{3,2,0,1:T(4,128)}), f32[1,128,4,128]{3,2,0,1:T(4,128)S(1)}, u32[]{:S(2)}, u32[]{:S(2)}) async-start(f32[1,128,4,128]{3,2,0,1:T(4,128)} %copy.161), calls=%async_computation.10 | async-start | bytes 524288 | tf_op jit(solution)/shard_map/all_to_all | solution.py:54
  440.2 15.0 %all-to-all-start.15 = ((f32[1,128,4,128]{3,2,0,1:T(4,128)}), f32[1,128,4,128]{3,2,0,1:T(4,128)S(1)}, u32[]{:S(2)}, u32[]{:S(2)}) async-start(f32[1,128,4,128]{3,2,0,1:T(4,128)} %copy.192), calls=%async_computation.15 | async-start | bytes 524288 | tf_op jit(solution)/shard_map/all_to_all | solution.py:55
  455.2 15.9 %all-to-all-start.14 = ((f32[1,128,4,128]{3,2,0,1:T(4,128)}), f32[1,128,4,128]{3,2,0,1:T(4,128)}, u32[]{:S(2)}, u32[]{:S(2)}) async-start(f32[1,128,4,128]{3,2,0,1:T(4,128)} %copy.187), calls=%async_computation.14 | async-start | bytes 524288 | tf_op jit(solution)/shard_map/all_to_all | solution.py:54
  472.1 1.0 copy-start.2
Sparse Core Ops, SparseCore 0:
  10.3 198.9 all-reduce.1
where the time goes:
time: 495 us; the launch traced here: 486 us
  waiting for transfers between devices  317 us (64%)
  starting transfers between devices  73.6 us (15%)
  matrix products  53.8 us (11%)
  local copies, waits for them, and re-layouts  23.8 us (5%)
  between operations  15.4 us (3%)
    psum x1, waiting for transfers between devices, broadcast(): return lax.psum(jnp.where(mine, value, jnp.zeros_like(value)), axis)  200 us
    dot_general x80, matrix products, along(): return jnp.einsum(form, field, table, precision=HIGH)  53.8 us
    all_to_all x4, waiting for transfers between devices, middle_section(): lax.all_to_all(imag_part, 'fft', split_axis=2, concat_axis=1, tiled=True)  33.8 us
    all_to_all x4, waiting for transfers between devices, middle_section(): lax.all_to_all(real_part, 'fft', split_axis=2, concat_axis=1, tiled=True)  30.7 us
    all_to_all x4, starting transfers between devices, middle_section(): lax.all_to_all(imag_part, 'fft', split_axis=2, concat_axis=1, tiled=True)  27.5 us
    all_to_all x4, waiting for transfers between devices, middle_section(): lax.all_to_all(imag_part, 'fft', split_axis=1, concat_axis=2, tiled=True)  26.2 us
    all_to_all x4, waiting for transfers between devices, middle_section(): lax.all_to_all(real_part, 'fft', split_axis=1, concat_axis=2, tiled=True)  26 us
    all_to_all x4, starting transfers between devices, middle_section(): lax.all_to_all(real_part, 'fft', split_axis=1, concat_axis=2, tiled=True)  15.9 us
  transfers between devices with their start and end apart: 17, of which 17 were waited for; matrix products, arithmetic and copies ran while one was open for 12% of the time, Pallas kernels for 0%

commit v1 on v0

v1 whole, which is shorter than its diff:
```python
import functools

import jax
import jax.numpy as jnp
import ml_dtypes
import numpy as np
from jax import lax
from jax.experimental import pallas as pl
from jax.experimental.pallas import tpu as pltpu
from jax.sharding import PartitionSpec as P

MESH = pl.DeviceIdType.MESH
N = 128
FFT = 32
TOP = 32767.0


def halves(table):
    high = table.astype(ml_dtypes.bfloat16)
    low = (table - high.astype(np.float64)).astype(ml_dtypes.bfloat16)
    return high, low


def tables():
    counter = np.arange(N)
    phase = (np.outer(counter, counter) % N) * (2.0 * np.pi / N)
    cosine, sine = np.cos(phase), np.sin(phase)
    forward = np.block([[cosine, sine], [-sine, cosine]])
    inverse = np.block([[cosine, -sine], [sine, cosine]]) / N
    to_columns = forward.reshape(2, FFT, 4, 2 * N).transpose(1, 0, 2, 3).reshape(2 * N, 2 * N)
    to_planes = inverse.reshape(2, FFT, 4, 2 * N).transpose(1, 2, 0, 3).reshape(2 * N, 2 * N)

    def left(table):
        high, low = halves(table)
        return np.concatenate([high, high, low], axis=1)

    def right(table):
        high, low = halves(table.T)
        return np.concatenate([high, high, low], axis=0)

    lefts = np.stack([left(to_columns), left(forward), left(to_planes), left(inverse)])
    rights = np.stack([right(forward), right(inverse)])
    return lefts, rights


def split(value):
    high = value.astype(jnp.bfloat16)
    low = (value - high.astype(jnp.float32)).astype(jnp.bfloat16)
    return high, low


def dot(a, b):
    return jnp.dot(a, b, preferred_element_type=jnp.float32)


def code(value, inverse_scale):
    ratio = value * inverse_scale
    root = ratio * lax.rsqrt(jnp.maximum(jnp.abs(ratio), 1e-30))
    return jnp.round(root * TOP).astype(jnp.int32).astype(jnp.int16)


def exchange_kernel(
    root_z,
    owner_ref, pair_ref, own_hbm, kernel_hbm, left_hbm, right_hbm,
    out_ref,
    own, table_l, table_r, weight, cand, block,
    send, recv, scale_out, scale_in,
    decoded, rhs, mid, product,
    load_sem, cand_send, cand_recv, ring_send, ring_recv, mate_send, mate_recv,
    data_send, data_recv, scale_send, scale_recv, own_sem,
):
    me = lax.axis_index("fft")
    group = lax.axis_index("band")
    y, z = lax.rem(group, 4), group // 4
    right_z, left_z = lax.rem(z + 1, 4) * 4 + y, lax.rem(z + 3, 4) * 4 + y

    loads = [
        pltpu.make_async_copy(own_hbm, own, load_sem.at[0]),
        pltpu.make_async_copy(left_hbm, table_l, load_sem.at[1]),
        pltpu.make_async_copy(right_hbm, table_r, load_sem.at[2]),
        pltpu.make_async_copy(kernel_hbm, weight, load_sem.at[3]),
    ]
    for load in loads:
        load.start()

    barrier = pltpu.get_barrier_semaphore()

    def mate(k):
        return z * 4 + lax.rem(y + k, 4)

    for k in range(1, 4):
        pl.semaphore_signal(barrier, inc=1, device_id={"band": mate(k)}, device_id_type=MESH)
    for other in (right_z, left_z):
        pl.semaphore_signal(barrier, inc=1, device_id={"band": other}, device_id_type=MESH)

    def greet(i, carry):
        pl.semaphore_signal(
            barrier, inc=1, device_id={"fft": lax.rem(me + i, FFT)}, device_id_type=MESH
        )
        return carry

    lax.fori_loop(1, FFT, greet, 0)
    pl.semaphore_wait(barrier, 5 + FFT - 1)

    def rows(half):
        return pl.ds(half * (N // 2), N // 2)

    def pass_on(p, half):
        there = right_z if half == 0 else left_z
        pltpu.make_async_remote_copy(
            block.at[p, y, rows(half)], block.at[p, y, rows(half)],
            ring_send, ring_recv.at[p, half],
            device_id={"band": there}, device_id_type=MESH,
        ).start()

    def arrived(p, half):
        here = block.at[p, y, rows(half)]
        pltpu.make_async_copy(here, here, ring_recv.at[p, half]).wait()

    def share(p, half):
        for k in range(1, 4):
            pltpu.make_async_remote_copy(
                block.at[p, y, rows(half)], block.at[p, y, rows(half)],
                mate_send, mate_recv.at[p],
                device_id={"band": mate(k)}, device_id_type=MESH,
            ).start()

    place = lax.rem(z - root_z + 4, 4)

    @pl.when(place == 0)
    def _():
        for p in range(4):
            for k in range(1, 4):
                there = lax.rem(y + k, 4)
                pltpu.make_async_remote_copy(
                    own_hbm.at[p, there], cand.at[p, y],
                    cand_send, cand_recv.at[p],
                    device_id={"band": mate(k)}, device_id_type=MESH,
                ).start()
        loads[0].wait()
        root_y = lax.rem(owner_ref[0], 4)
        for p in range(4):
            cand[p, y] = own[p, y]
            pltpu.make_async_copy(
                cand.at[p, pl.ds(0, 3)], cand.at[p, pl.ds(0, 3)], cand_recv.at[p]
            ).wait()
            chosen = cand[p, 0]
            for k in range(1, 4):
                chosen = jnp.where(root_y == k, cand[p, k], chosen)
            block[p, y] = chosen
            pass_on(p, 0)
            pass_on(p, 1)
            share(p, 0)
            share(p, 1)
        pltpu.make_async_copy(cand.at[:, pl.ds(0, 3)], cand.at[:, pl.ds(0, 3)], cand_send).wait()

    @pl.when(place == 1)
    def _():
        for p in range(4):
            arrived(p, 0)
            pass_on(p, 0)
            share(p, 0)
        for p in range(4):
            arrived(p, 1)
            share(p, 1)
        loads[0].wait()

    @pl.when(place == 2)
    def _():
        for p in range(4):
            for half in range(2):
                arrived(p, half)
                pass_on(p, half)
                share(p, half)
        loads[0].wait()

    @pl.when(place == 3)
    def _():
        for p in range(4):
            arrived(p, 1)
            pass_on(p, 1)
            share(p, 1)
        for p in range(4):
            arrived(p, 0)
            share(p, 0)
        loads[0].wait()

    for load in loads[1:]:
        load.wait()

    def own_band(p):
        band = jnp.int32(0)
        for j in range(1, 4):
            band = jnp.where(pair_ref[0, j] == p, j, band)
        return band

    def ship(step, f):
        pltpu.make_async_copy(
            send.at[step, f, me], recv.at[step, f, me], own_sem.at[step, f]
        ).start()

        def one(i, carry):
            there = lax.rem(me + i, FFT)
            pltpu.make_async_remote_copy(
                send.at[step, f, there], recv.at[step, f, me],
                data_send.at[step, f], data_recv.at[step, f],
                device_id={"fft": there}, device_id_type=MESH,
            ).start()
            pltpu.make_async_remote_copy(
                scale_out.at[step, f], scale_in.at[step, f, me],
                scale_send.at[step, f], scale_recv.at[step, f],
                device_id={"fft": there}, device_id_type=MESH,
            ).start()
            return carry

        lax.fori_loop(1, FFT, one, 0)

    def landed(step, f):
        most = pl.ds(0, FFT - 1)
        for buffer, sem in ((recv, data_recv), (scale_in, scale_recv)):
            here = buffer.at[step, f, most]
            pltpu.make_async_copy(here, here, sem.at[step, f]).wait()
        here = recv.at[step, f, 0]
        pltpu.make_async_copy(here, here, own_sem.at[step, f]).wait()

    def encode(step, f, pieces):
        top = jnp.max(jnp.abs(pieces[0]), axis=0, keepdims=True)
        for piece in pieces[1:]:
            top = jnp.maximum(top, jnp.max(jnp.abs(piece), axis=0, keepdims=True))
        top = jnp.maximum(jnp.max(top, axis=1, keepdims=True), 1e-36)
        inverse_scale = 1.0 / top
        scale = jnp.broadcast_to(top * (1.0 / (TOP * TOP)), (1, N))
        scale_out[step, f] = scale
        scale_in[step, f, me] = scale
        for pair in range(2):
            both = jnp.concatenate(
                [pieces[2 * pair].reshape(FFT, 8, N), pieces[2 * pair + 1].reshape(FFT, 8, N)],
                axis=1,
            )
            send[step, f, :, pair] = code(both, inverse_scale)

    def decode(step, f):
        raw = recv[step, f].astype(jnp.int32).astype(jnp.float32)
        value = raw * jnp.abs(raw) * scale_in[step, f].reshape(FFT, 1, 1, N)
        decoded[...] = value.reshape(FFT * 32, N)

    def line(row):
        return decoded[pl.ds(row, N, stride=8), :]

    def put(row, column, value):
        high, low = split(value)
        at = pl.ds(column, value.shape[1])
        rhs[pl.ds(row, N), at] = high
        rhs[pl.ds(row + 2 * N, N), at] = low
        rhs[pl.ds(row + 4 * N, N), at] = high

    def forward(f):
        for p in (2 * f, 2 * f + 1):
            others = block.at[p, pl.ds(0, 3)]
            pltpu.make_async_copy(others, others, mate_recv.at[p]).wait()
        densities = []
        for p in (2 * f, 2 * f + 1):
            density = block[p].astype(jnp.float32) * own[own_band(p)].astype(jnp.float32)
            densities.append(split(density.reshape(4 * N, N)))
        (high_0, low_0), (high_1, low_1) = densities
        lhs = jnp.concatenate([high_0, high_1, low_0, low_1, high_0, high_1], axis=1)
        mid[...] = dot(lhs, table_r[0])
        pieces = []
        for pair in range(2):
            for second in range(2):
                for part in range(2):
                    at = pl.ds((2 * pair + second) * N, N)
                    put(part * N, second * N, mid[at, pl.ds(part * N, N)])
            result = dot(table_l[0], rhs[:, pl.ds(0, 2 * N)])
            pieces += [result[:, :N], result[:, N:]]
        encode(0, f, pieces)
        ship(0, f)

    def middle(f):
        landed(0, f)
        decode(0, f)
        for part in range(2):
            for r in range(4):
                put(part * N, r * N, line(part * 4 + r))
        spectrum = dot(table_l[1], rhs[...])
        for r in range(4):
            factor = weight[pl.ds(r, N, stride=4), :]
            for part in range(2):
                put(part * N, r * N, spectrum[part * N : (part + 1) * N, r * N : (r + 1) * N] * factor)
        result = dot(table_l[2], rhs[...])
        encode(1, f, [result[:, r * N : (r + 1) * N] for r in range(4)])
        ship(1, f)

    def backward(f):
        landed(1, f)
        decode(1, f)
        for pair in range(2):
            for second in range(2):
                for part in range(2):
                    put(part * N, second * N, line((2 * pair + second) * 2 + part))
            field = dot(table_l[3], rhs[:, pl.ds(0, 2 * N)])
            lhs = []
            for second in range(2):
                at = slice(second * N, (second + 1) * N)
                high_0, low_0 = split(field[:N, at])
                high_1, low_1 = split(field[N:, at])
                lhs.append(jnp.concatenate([high_0, high_1, low_0, low_1, high_0, high_1], axis=1))
            potential = dot(jnp.concatenate(lhs, axis=0), table_r[1])
            for part in range(2):
                p = 2 * f + part
                at = pl.ds(2 * pair, 2)
                partner = block[p, at].astype(jnp.float32)
                product[p, at] = -(partner * potential[:, part * N : (part + 1) * N].reshape(2, N, N))

    forward(0)
    forward(1)
    middle(0)
    middle(1)
    backward(0)
    backward(1)

    for j in range(4):
        out_ref[j] = product[pair_ref[0, j]]

    @pl.when(place == 0)
    def _():
        here = block.at[:, 0]
        pltpu.make_async_copy(here, here, ring_send).wait()

    @pl.when(place == 2)
    def _():
        here = block.at[:, 0]
        pltpu.make_async_copy(here, here, ring_send).wait()

    @pl.when(lax.rem(place, 2) == 1)
    def _():
        here = block.at[:, 0, rows(0)]
        pltpu.make_async_copy(here, here, ring_send).wait()

    here = block.at[:, pl.ds(0, 3)]
    pltpu.make_async_copy(here, here, mate_send).wait()
    for step in range(2):
        for f in range(2):
            here = send.at[step, f, pl.ds(0, FFT - 1)]
            pltpu.make_async_copy(here, here, data_send.at[step, f]).wait()
            here = scale_in.at[step, f, pl.ds(0, FFT - 1)]
            pltpu.make_async_copy(here, here, scale_send.at[step, f]).wait()


def call(root_z, owner, pairing, orbitals, kernel, lefts, rights):
    anywhere = pl.BlockSpec(memory_space=pl.ANY)
    scalars = pl.BlockSpec(memory_space=pltpu.SMEM)
    dma = pltpu.SemaphoreType.DMA
    return pl.pallas_call(
        functools.partial(exchange_kernel, root_z),
        out_shape=jax.ShapeDtypeStruct((4, 4, N, N), jnp.float32),
        in_specs=[scalars, scalars, anywhere, anywhere, anywhere, anywhere],
        out_specs=pl.BlockSpec(memory_space=pltpu.VMEM),
        scratch_shapes=[
            pltpu.VMEM((4, 4, N, N), jnp.bfloat16),
            pltpu.VMEM((4, 2 * N, 6 * N), jnp.bfloat16),
            pltpu.VMEM((2, 6 * N, 2 * N), jnp.bfloat16),
            pltpu.VMEM((4 * N, N), jnp.float32),
            pltpu.VMEM((4, 4, N, N), jnp.bfloat16),
            pltpu.VMEM((4, 4, N, N), jnp.bfloat16),
            pltpu.VMEM((2, 2, FFT, 2, 16, N), jnp.int16),
            pltpu.VMEM((2, 2, FFT, 2, 16, N), jnp.int16),
            pltpu.VMEM((2, 2, 1, N), jnp.float32),
            pltpu.VMEM((2, 2, FFT, 1, N), jnp.float32),
            pltpu.VMEM((FFT * 32, N), jnp.float32),
            pltpu.VMEM((6 * N, 4 * N), jnp.bfloat16),
            pltpu.VMEM((4 * N, 2 * N), jnp.float32),
            pltpu.VMEM((4, 4, N, N), jnp.float32),
            dma((4,)),
            dma,
            dma((4,)),
            dma,
            dma((4, 2)),
            dma,
            dma((4,)),
            dma((2, 2)),
            dma((2, 2)),
            dma((2, 2)),
            dma((2, 2)),
            dma((2, 2)),
        ],
        compiler_params=pltpu.CompilerParams(
            collective_id=root_z, has_side_effects=True, vmem_limit_bytes=48 * 1024 * 1024
        ),
    )(owner, pairing, orbitals, kernel, lefts, rights)


def local(orbitals, kernel, pairing, owner):
    lefts, rights = tables()
    root_z = (owner[0] % 16) // 4
    return lax.switch(
        root_z,
        [functools.partial(call, k) for k in range(4)],
        owner, pairing, orbitals, kernel.reshape(4 * N, N), jnp.asarray(lefts), jnp.asarray(rights),
    )


def solution(mesh):
    placed = (P("band", "fft", None, None), P(None, "fft", None), P("band", None), P())
    return jax.shard_map(
        local, mesh=mesh, in_specs=placed, out_specs=P("band", "fft", None, None), check_vma=False
    )
```

time: 495 us -> 70.2 us (0.14); the launches traced: 486 us -> 70 us
  waiting for transfers between devices: 317 us -> 0 us
  starting transfers between devices: 73.6 us -> 0 us
  Pallas kernels: 0 us -> 67.8 us
  matrix products: 53.8 us -> 0 us
  local copies, waits for them, and re-layouts: 23.8 us -> 0.97 us
  between operations: 15.4 us -> 0.7 us
    psum x1 -> x0, waiting for transfers between devices: 200 us -> none  [broadcast(): return lax.psum(jnp.where(mine, value, jnp.zeros_like(value)), axis)]
    all_to_all x16 -> x0, waiting for transfers between devices: 117 us -> none  [the longest x4 33.8 us: middle_section(): lax.all_to_all(imag_part, 'fft', split_axis=2, concat_axis=1, tiled=True)]
    all_to_all x16 -> x0, starting transfers between devices: 73.6 us -> none  [the longest x4 27.5 us: middle_section(): lax.all_to_all(imag_part, 'fft', split_axis=2, concat_axis=1, tiled=True)]
    pallas_call x0 -> x1, Pallas kernels: none -> 67.8 us  [call(): pl.pallas_call(functools.partial(exchange_kernel, root_z), out_shape=jax....]
    dot_general x80 -> x0, matrix products: 53.8 us -> none  [along(): return jnp.einsum(form, field, table, precision=HIGH)]
    mul x8 -> x0, local copies, waits for them, and re-layouts: 7.06 us -> none  [the longest x4 3.54 us: inverse_pair(): (along(form, real_part, cosine_table) - along(form, imag_part, sine_table...]
    unnamed x24 -> x1, local copies, waits for them, and re-layouts: 6.36 us -> 0.97 us
  transfers between devices with their start and end apart: 17 -> 0, of which waited for: 17 -> 0; matrix products, arithmetic and copies ran while one was open for 12% -> 0% of each run, Pallas kernels for 0% -> 0%
where the time goes in v1:
time: 70.2 us; the launch traced here: 70 us
  Pallas kernels  67.8 us (97%)
  local copies, waits for them, and re-layouts  0.97 us (1%)
    pallas_call x1, Pallas kernels, call(): pl.pallas_call(functools.partial(exchange_kernel, root_z), out_shape=jax....  67.8 us

profile of v1, /device:TPU:1, one launch (start us, length us, event | category | flops | bytes accessed | tf_op | source)
XLA Modules:
  0.0 70.0 jit_solution(18343381308522335106)
XLA Ops:
  0.7 68.4 %conditional.1 = (f32[4,4,128,128]{3,2,1,0:T(8,128)S(1)}) conditional(s32[]{:T(128)} %clamp.3, (s32[1]{0:T(128)}, s32[1,4]{1,0:T(1,128)}, bf16[4,4,128,128]{3,2,1,0:T(8,128)(2,1)}, f32[512,128]{1,0:T(8,128)}, bf16[4,256,768]{2,1,0:T(8,128)(2,1)}, /*index=5*/bf16[2,768,256]{2,1,0:T(8,128)(2,1)}) %tuple.26, ...), branch_computations={%region_0.1_spmd, %region_1.2_spmd, %region_2.3_spmd, %region_3.4_... | conditional | bytes 8 | solution.py:396
  0.7 67.8 %branch_1_fun.1 = f32[4,4,128,128]{3,2,1,0:T(8,128)S(1)} custom-call(s32[1]{0:T(128)} %get-tuple-element.64.owner_ref, s32[1,4]{1,0:T(1,128)} %get-tuple-element.65.pair_ref, bf16[4,4,128,128]{3,2,1,0:T(8,128)(2,1)} %get-tuple-element.66.own_hbm, f32[512,128]{1,0:T(8,128)} %get-tuple-element.67.kernel_hbm, bf16[4,256,768]{2,1,0:T(8,128)(2,1)} %get-tuple-element.68.left_hbm, ...), custom_call_target="tpu_custom_call" | custom-call | tf_op jit(solution)/shard_map/cond/branch_1_fun/pallas_call | solution.py:354
  69.1 1.0 %copy.17 = f32[4,4,128,128]{3,2,1,0:T(8,128)} copy(f32[4,4,128,128]{3,2,1,0:T(8,128)S(1)} %get-tuple-element.82) | data formatting | bytes 2097152

commit v2 on v1

--- a/solution.py
+++ b/solution.py
@@ -13,6 +13,28 @@
 N = 128
 FFT = 32
 TOP = 32767.0
+DEPTH = 1
+RIGHT, LEFT = 0, 1
+STEP = 3
+
+
+def plan(root):
+    ring = ((RIGHT,) * 3, (LEFT,) * 3)
+    lines = {
+        0: tuple(enumerate(ring)),
+        1: ((0, (RIGHT,) * 2), (0, (LEFT,)), (1, (LEFT,) * 3)),
+        2: tuple(enumerate(ring)),
+        3: ((0, (RIGHT,) * 3), (1, (LEFT,) * 2), (1, (RIGHT,))),
+    }[root]
+    routes = [[] for _ in range(4)]
+    steps = [[0, 0] for _ in range(4)]
+    for half, ways in lines:
+        at = root
+        for step, way in enumerate(ways):
+            routes[at].append((half, way))
+            at = (at + (1 if way == RIGHT else 3)) % 4
+            steps[at][half] = step + 1
+    return routes, steps
 
 
 def halves(table):
@@ -69,6 +91,7 @@
     load_sem, cand_send, cand_recv, ring_send, ring_recv, mate_send, mate_recv,
     data_send, data_recv, scale_send, scale_recv, own_sem,
 ):
+    routes, steps = plan(root_z)
     me = lax.axis_index("fft")
     group = lax.axis_index("band")
     y, z = lax.rem(group, 4), group // 4
@@ -105,84 +128,82 @@
     def rows(half):
         return pl.ds(half * (N // 2), N // 2)
 
-    def pass_on(p, half):
-        there = right_z if half == 0 else left_z
-        pltpu.make_async_remote_copy(
-            block.at[p, y, rows(half)], block.at[p, y, rows(half)],
-            ring_send, ring_recv.at[p, half],
+    def piece(p, half):
+        return block.at[p, y, rows(half)]
+
+    def pass_on(p, half, way):
+        there = right_z if way == RIGHT else left_z
+        return pltpu.make_async_remote_copy(
+            piece(p, half), piece(p, half),
+            ring_send.at[p, half, way], ring_recv.at[p, half],
             device_id={"band": there}, device_id_type=MESH,
-        ).start()
-
-    def arrived(p, half):
-        here = block.at[p, y, rows(half)]
-        pltpu.make_async_copy(here, here, ring_recv.at[p, half]).wait()
+        )
 
     def share(p, half):
         for k in range(1, 4):
             pltpu.make_async_remote_copy(
-                block.at[p, y, rows(half)], block.at[p, y, rows(half)],
+                piece(p, half), piece(p, half),
                 mate_send, mate_recv.at[p],
                 device_id={"band": mate(k)}, device_id_type=MESH,
             ).start()
 
+    def spread(p):
+        for k in range(1, 4):
+            there = lax.rem(y + k, 4)
+            pltpu.make_async_remote_copy(
+                own_hbm.at[p, there], cand.at[p, y],
+                cand_send, cand_recv.at[p],
+                device_id={"band": mate(k)}, device_id_type=MESH,
+            ).start()
+
     place = lax.rem(z - root_z + 4, 4)
 
     @pl.when(place == 0)
     def _():
-        for p in range(4):
-            for k in range(1, 4):
-                there = lax.rem(y + k, 4)
-                pltpu.make_async_remote_copy(
-                    own_hbm.at[p, there], cand.at[p, y],
-                    cand_send, cand_recv.at[p],
-                    device_id={"band": mate(k)}, device_id_type=MESH,
-                ).start()
+        eager = root_z == 0
+        for p in range(4 if eager else 2):
+            spread(p)
         loads[0].wait()
         root_y = lax.rem(owner_ref[0], 4)
         for p in range(4):
             cand[p, y] = own[p, y]
-            pltpu.make_async_copy(
-                cand.at[p, pl.ds(0, 3)], cand.at[p, pl.ds(0, 3)], cand_recv.at[p]
-            ).wait()
+        for p in range(4):
+            three = cand.at[p, pl.ds(0, 3)]
+            pltpu.make_async_copy(three, three, cand_recv.at[p]).wait()
+            if p < 2 and not eager:
+                spread(p + 2)
             chosen = cand[p, 0]
             for k in range(1, 4):
                 chosen = jnp.where(root_y == k, cand[p, k], chosen)
             block[p, y] = chosen
-            pass_on(p, 0)
-            pass_on(p, 1)
+            for half, way in routes[root_z]:
+                if p >= DEPTH:
+                    pass_on(p - DEPTH, half, way).wait_send()
+                pass_on(p, half, way).start()
+            if eager:
+                share(p, 0)
+                share(p, 1)
+        for p in () if eager else range(4):
             share(p, 0)
             share(p, 1)
-        pltpu.make_async_copy(cand.at[:, pl.ds(0, 3)], cand.at[:, pl.ds(0, 3)], cand_send).wait()
-
-    @pl.when(place == 1)
+        three = cand.at[:, pl.ds(0, 3)]
+        pltpu.make_async_copy(three, three, cand_send).wait()
+
+    def relay(here):
+        order = [(steps[here][half] * STEP + p, p, half) for p in range(4) for half in range(2)]
+        for _, p, half in sorted(order):
+            pltpu.make_async_copy(piece(p, half), piece(p, half), ring_recv.at[p, half]).wait()
+            for which, way in routes[here]:
+                if which == half:
+                    pass_on(p, half, way).start()
+            share(p, half)
+
+    for here in range(4):
+        if here != root_z:
+            pl.when(z == here)(functools.partial(relay, here))
+
+    @pl.when(place != 0)
     def _():
-        for p in range(4):
-            arrived(p, 0)
-            pass_on(p, 0)
-            share(p, 0)
-        for p in range(4):
-            arrived(p, 1)
-            share(p, 1)
-        loads[0].wait()
-
-    @pl.when(place == 2)
-    def _():
-        for p in range(4):
-            for half in range(2):
-                arrived(p, half)
-                pass_on(p, half)
-                share(p, half)
-        loads[0].wait()
-
-    @pl.when(place == 3)
-    def _():
-        for p in range(4):
-            arrived(p, 1)
-            pass_on(p, 1)
-            share(p, 1)
-        for p in range(4):
-            arrived(p, 0)
-            share(p, 0)
         loads[0].wait()
 
     for load in loads[1:]:
@@ -322,20 +343,14 @@
     for j in range(4):
         out_ref[j] = product[pair_ref[0, j]]
 
-    @pl.when(place == 0)
-    def _():
-        here = block.at[:, 0]
-        pltpu.make_async_copy(here, here, ring_send).wait()
-
-    @pl.when(place == 2)
-    def _():
-        here = block.at[:, 0]
-        pltpu.make_async_copy(here, here, ring_send).wait()
-
-    @pl.when(lax.rem(place, 2) == 1)
-    def _():
-        here = block.at[:, 0, rows(0)]
-        pltpu.make_async_copy(here, here, ring_send).wait()
+    def sent(here):
+        for p in range(4 - DEPTH if here == root_z else 0, 4):
+            for half, way in routes[here]:
+                pass_on(p, half, way).wait_send()
+
+    for here in range(4):
+        if routes[here]:
+            pl.when(z == here)(functools.partial(sent, here))
 
     here = block.at[:, pl.ds(0, 3)]
     pltpu.make_async_copy(here, here, mate_send).wait()
@@ -374,7 +389,7 @@
             dma((4,)),
             dma,
             dma((4,)),
-            dma,
+            dma((4, 2, 2)),
             dma((4, 2)),
             dma,
             dma((4,)),

time: 70.2 us -> 66.7 us (0.950)
  Pallas kernels: 67.8 us -> 64.3 us
    pallas_call x1, Pallas kernels: 67.8 us -> 64.3 us  [call(): pl.pallas_call(functools.partial(exchange_kernel, root_z), out_shape=jax....]
where the time goes in v2:
time: 66.7 us; the launch traced here: 66.5 us
  Pallas kernels  64.3 us (96%)
  local copies, waits for them, and re-layouts  0.97 us (1%)
  between operations  0.7 us (1%)
    pallas_call x1, Pallas kernels, call(): pl.pallas_call(functools.partial(exchange_kernel, root_z), out_shape=jax....  64.3 us

profile of v2, /device:TPU:1, one launch (start us, length us, event | category | flops | bytes accessed | tf_op | source)
XLA Modules:
  0.0 66.5 jit_solution(2459788871921801927)
XLA Ops:
  0.7 64.8 %conditional.1 = (f32[4,4,128,128]{3,2,1,0:T(8,128)S(1)}) conditional(s32[]{:T(128)} %clamp.3, (s32[1]{0:T(128)}, s32[1,4]{1,0:T(1,128)}, bf16[4,4,128,128]{3,2,1,0:T(8,128)(2,1)}, f32[512,128]{1,0:T(8,128)}, bf16[4,256,768]{2,1,0:T(8,128)(2,1)}, /*index=5*/bf16[2,768,256]{2,1,0:T(8,128)(2,1)}) %tuple.26, ...), branch_computations={%region_0.1_spmd, %region_1.2_spmd, %region_2.3_spmd, %region_3.4_... | conditional | bytes 8 | solution.py:411
  0.9 64.3 %branch_3_fun.1 = f32[4,4,128,128]{3,2,1,0:T(8,128)S(1)} custom-call(s32[1]{0:T(128)} %get-tuple-element.76.owner_ref, s32[1,4]{1,0:T(1,128)} %get-tuple-element.77.pair_ref, bf16[4,4,128,128]{3,2,1,0:T(8,128)(2,1)} %get-tuple-element.78.own_hbm, f32[512,128]{1,0:T(8,128)} %get-tuple-element.79.kernel_hbm, bf16[4,256,768]{2,1,0:T(8,128)(2,1)} %get-tuple-element.80.left_hbm, ...), custom_call_target="tpu_custom_call" | custom-call | tf_op jit(solution)/shard_map/cond/branch_3_fun/pallas_call | solution.py:369
  65.5 1.0 %copy.17 = f32[4,4,128,128]{3,2,1,0:T(8,128)} copy(f32[4,4,128,128]{3,2,1,0:T(8,128)S(1)} %get-tuple-element.82) | data formatting | bytes 2097152

commit v3 on v2

--- a/solution.py
+++ b/solution.py
@@ -101,7 +101,7 @@
         pltpu.make_async_copy(own_hbm, own, load_sem.at[0]),
         pltpu.make_async_copy(left_hbm, table_l, load_sem.at[1]),
         pltpu.make_async_copy(right_hbm, table_r, load_sem.at[2]),
-        pltpu.make_async_copy(kernel_hbm, weight, load_sem.at[3]),
+        pltpu.make_async_copy(kernel_hbm, weight.at[pl.ds(0, 4 * N)], load_sem.at[3]),
     ]
     for load in loads:
         load.start()
@@ -263,7 +263,7 @@
     def decode(step, f):
         raw = recv[step, f].astype(jnp.int32).astype(jnp.float32)
         value = raw * jnp.abs(raw) * scale_in[step, f].reshape(FFT, 1, 1, N)
-        decoded[...] = value.reshape(FFT * 32, N)
+        decoded[pl.ds(0, FFT * 32), :] = value.reshape(FFT * 32, N)
 
     def line(row):
         return decoded[pl.ds(row, N, stride=8), :]
@@ -375,14 +375,14 @@
             pltpu.VMEM((4, 4, N, N), jnp.bfloat16),
             pltpu.VMEM((4, 2 * N, 6 * N), jnp.bfloat16),
             pltpu.VMEM((2, 6 * N, 2 * N), jnp.bfloat16),
-            pltpu.VMEM((4 * N, N), jnp.float32),
+            pltpu.VMEM((4 * N + 8, N), jnp.float32),
             pltpu.VMEM((4, 4, N, N), jnp.bfloat16),
             pltpu.VMEM((4, 4, N, N), jnp.bfloat16),
             pltpu.VMEM((2, 2, FFT, 2, 16, N), jnp.int16),
             pltpu.VMEM((2, 2, FFT, 2, 16, N), jnp.int16),
             pltpu.VMEM((2, 2, 1, N), jnp.float32),
             pltpu.VMEM((2, 2, FFT, 1, N), jnp.float32),
-            pltpu.VMEM((FFT * 32, N), jnp.float32),
+            pltpu.VMEM((FFT * 32 + 8, N), jnp.float32),
             pltpu.VMEM((6 * N, 4 * N), jnp.bfloat16),
             pltpu.VMEM((4 * N, 2 * N), jnp.float32),
             pltpu.VMEM((4, 4, N, N), jnp.float32),

time: 66.7 us -> 65.2 us (0.978)
  the two profiles are of different devices: /device:TPU:1 before, /device:TPU:129 now
where the time goes in v3:
time: 65.2 us; the launch traced here: 65.1 us
  Pallas kernels  62.9 us (96%)
  local copies, waits for them, and re-layouts  0.97 us (1%)
  between operations  0.7 us (1%)
    pallas_call x1, Pallas kernels, call(): pl.pallas_call(functools.partial(exchange_kernel, root_z), out_shape=jax....  62.9 us

profile of v3, /device:TPU:129, one launch (start us, length us, event | category | flops | bytes accessed | tf_op | source)
XLA Modules:
  0.0 65.1 jit_solution(12687952669937838441)
XLA Ops:
  0.7 63.5 %conditional.1 = (f32[4,4,128,128]{3,2,1,0:T(8,128)S(1)}) conditional(s32[]{:T(128)} %clamp.3, (s32[1]{0:T(128)}, s32[1,4]{1,0:T(1,128)}, bf16[4,4,128,128]{3,2,1,0:T(8,128)(2,1)}, f32[512,128]{1,0:T(8,128)}, bf16[4,256,768]{2,1,0:T(8,128)(2,1)}, /*index=5*/bf16[2,768,256]{2,1,0:T(8,128)(2,1)}) %tuple.26, ...), branch_computations={%region_0.1_spmd, %region_1.2_spmd, %region_2.3_spmd, %region_3.4_... | conditional | bytes 8 | solution.py:411
  0.9 62.9 %branch_3_fun.1 = f32[4,4,128,128]{3,2,1,0:T(8,128)S(1)} custom-call(s32[1]{0:T(128)} %get-tuple-element.76.owner_ref, s32[1,4]{1,0:T(1,128)} %get-tuple-element.77.pair_ref, bf16[4,4,128,128]{3,2,1,0:T(8,128)(2,1)} %get-tuple-element.78.own_hbm, f32[512,128]{1,0:T(8,128)} %get-tuple-element.79.kernel_hbm, bf16[4,256,768]{2,1,0:T(8,128)(2,1)} %get-tuple-element.80.left_hbm, ...), custom_call_target="tpu_custom_call" | custom-call | tf_op jit(solution)/shard_map/cond/branch_3_fun/pallas_call | solution.py:369
  64.1 1.0 %copy.17 = f32[4,4,128,128]{3,2,1,0:T(8,128)} copy(f32[4,4,128,128]{3,2,1,0:T(8,128)S(1)} %get-tuple-element.82) | data formatting | bytes 2097152
